TPU v7x, 256 devices: a whole 4x4x8 slice. The times are simulated.
256 devices in a mesh: dp: 64 (over z, x, core), tp: 4 (over y).
Axes of the slice: x: 4, y: 4, z: 8, core: 2. Of those that a mesh axis runs over, the one named last changes fastest.
Arguments:
- hidden: bfloat16 [2048, 4096], P('dp', 'tp'), may hold values from -6 to 6
- routes: int32 [2048, 8], P('dp'), may hold values from 0 to 63, all different within a row; in each aligned block of 32 rows (0 to 31, 32 to 63, ...) at most 8 rows name the same one
- routing_weights: float32 [2048, 8], P('dp'), may hold values from 0.05 to 1
- w_gate: bfloat16 [64, 4096, 1536], P('dp', None, 'tp'), may hold values from -0.09375 to 0.09375
- w_up: bfloat16 [64, 4096, 1536], P('dp', None, 'tp'), may hold values from -0.09375 to 0.09375
- w_down: bfloat16 [64, 1536, 4096], P('dp', 'tp'), may hold values from -0.15625 to 0.15625
- norm_gain: float32 [4096], replicated, may hold values from 0.1 to 1.9
- key_projection_weight: bfloat16 [4096, 512], P(None, 'tp'), may hold values from -0.09375 to 0.09375
- value_projection_weight: bfloat16 [4096, 512], P(None, 'tp'), may hold values from -0.09375 to 0.09375
- queries: bfloat16 [2048, 8192], P('dp', 'tp'), may hold values from -128 to 128
- cached_key_rows: bfloat16 [64, 128, 512], P('dp', None, 'tp'), may hold values from -4 to 4
- cached_value_rows: bfloat16 [64, 128, 512], P('dp', None, 'tp'), may hold values from -6 to 6
- lengths: int32 [64], P('dp'), may hold values from 16 to 128
- parents: int32 [64, 32], P('dp'), may hold values from -1 to 30, as said below
Outputs:
- layer_output: bfloat16 [2048, 4096], P('dp', 'tp')
- next_layer_keys: bfloat16 [2048, 512], P('dp', 'tp')
- next_layer_values: bfloat16 [2048, 512], P('dp', 'tp')
- attended: bfloat16 [2048, 8192], P('dp', 'tp')
Inputs may be any that keep to these rules, and one draw needn't show every extreme that they name: `routes`: each row names 8 different experts. In each aligned block of 32 rows (the rows of one device) no expert is named by more than 8 rows, a bound that some block reaches. `parents`: node 0 of each request is the root, with parent -1; every other node i has its parent among nodes max(0, i - 8) to i - 1.
All inputs are finite; a program needn't handle non-finite values.
Results may differ from a plain program's by a relative error of at most 0.013.
Values may be sent and summed in bfloat16 or wider, within the bound.
No kernel may reach another device: no remote copies, remote signals or barrier semaphores. Data moves between devices by JAX's collectives and lax.ppermute only.
A program may use at most 64 MiB of HBM per device.

v0:
```python
import math
import jax
import jax.numpy as jnp
from jax import lax
from jax.sharding import PartitionSpec as P

HEAD_SIZE = 128


def split_up(shard, dim, size):
    shape = shard.shape
    tiles = shard.reshape(*shape[:dim], size, shape[dim] // size, *shape[dim + 1 :])
    return jnp.moveaxis(tiles, dim, 0)


def sent_and_summed(shard, axis, dim):
    size = lax.axis_size(axis)
    tiles = lax.all_to_all(split_up(shard, dim, size), axis, 0, 0, tiled=True)
    return jnp.sum(tiles.astype(jnp.float32), axis=0)


def joined_along(tiles, dim):
    shape = list(tiles.shape[1:])
    shape[dim] *= tiles.shape[0]
    return jnp.moveaxis(tiles, 0, dim).reshape(shape)


def copy_for_each(shard, axis):
    copies = jnp.broadcast_to(shard, (lax.axis_size(axis), *shard.shape))
    return lax.all_to_all(copies, axis, split_axis=0, concat_axis=0, tiled=True)


def gathered_copies(shard, axis, dim):
    return joined_along(copy_for_each(shard, axis), dim)


def ancestry(parent_row):
    node_count = parent_row.shape[0]
    position = jnp.arange(node_count, dtype=jnp.int32)
    reached = (parent_row[:, None] == position[None, :]).astype(jnp.float32)
    reached = reached + jnp.eye(node_count, dtype=jnp.float32)
    for doubling in range((node_count - 1).bit_length()):
        reached = jnp.minimum(jnp.dot(reached, reached, preferred_element_type=jnp.float32), 1.0)
    return reached > 0.5


def quarter_to_whole(received):
    return lax.all_gather(received, "tp", axis=2, tiled=True)


def attend_local(
    queries, cached_key_rows, cached_value_rows, tree_key_rows, tree_value_rows, lengths, parents
):
    request_count = lengths.shape[0]
    node_count = parents.shape[1]
    slot_length = cached_key_rows.shape[1]
    kv_local = cached_key_rows.shape[2] // HEAD_SIZE
    query_group_count = queries.shape[1] // (kv_local * HEAD_SIZE)
    scaled = 1.0 / math.sqrt(HEAD_SIZE)
    tree_query_block = queries.reshape(
        request_count, node_count, kv_local, query_group_count, HEAD_SIZE
    )
    joined_key_block = cached_key_rows.reshape(request_count, slot_length, kv_local, HEAD_SIZE)
    joined_value_block = cached_value_rows.reshape(request_count, slot_length, kv_local, HEAD_SIZE)
    tree_key_block = tree_key_rows.reshape(request_count, node_count, kv_local, HEAD_SIZE)
    tree_value_block = tree_value_rows.reshape(request_count, node_count, kv_local, HEAD_SIZE)
    cache_scores = (
        jnp.einsum(
            "rnkgd,rpkd->rkgnp",
            tree_query_block,
            joined_key_block,
            preferred_element_type=jnp.float32,
        )
        * scaled
    )
    tree_scores = (
        jnp.einsum(
            "rnkgd,rmkd->rkgnm",
            tree_query_block,
            tree_key_block,
            preferred_element_type=jnp.float32,
        )
        * scaled
    )
    visible = jnp.arange(slot_length, dtype=jnp.int32)[None, :] < lengths[:, None]
    cache_scores = jnp.where(visible[:, None, None, None, :], cache_scores, -1e30)
    related = jax.vmap(ancestry)(parents)
    tree_scores = jnp.where(related[:, None, None], tree_scores, -1e30)
    highest = jnp.maximum(jnp.max(cache_scores, axis=-1), jnp.max(tree_scores, axis=-1))[..., None]
    cache_raised = jnp.exp(cache_scores - highest)
    tree_raised = jnp.exp(tree_scores - highest)
    denominator = jnp.sum(cache_raised, axis=-1, keepdims=True) + jnp.sum(
        tree_raised, axis=-1, keepdims=True
    )
    cache_weights = (cache_raised / denominator).astype(jnp.bfloat16)
    tree_weights = (tree_raised / denominator).astype(jnp.bfloat16)
    output = jnp.einsum(
        "rkgnp,rpkd->rnkgd", cache_weights, joined_value_block, preferred_element_type=jnp.float32
    )
    output = output + jnp.einsum(
        "rkgnm,rmkd->rnkgd", tree_weights, tree_value_block, preferred_element_type=jnp.float32
    )
    return output.reshape(request_count * node_count, -1).astype(jnp.bfloat16)


def on_device(
    hidden,
    routes,
    routing_weights,
    w_gate,
    w_up,
    w_down,
    norm_gain,
    key_projection_weight,
    value_projection_weight,
    queries,
    cached_key_rows,
    cached_value_rows,
    lengths,
    parents,
):
    token_count = hidden.shape[0]
    top_count = routes.shape[1]
    local_experts = w_gate.shape[0]
    expert_count = lax.axis_size("dp") * local_experts
    capacity = min(token_count, 2 * token_count * top_count // expert_count)
    column_count = hidden.shape[1]
    weights = routing_weights / jnp.sum(routing_weights, axis=1, keepdims=True)
    expert_ids = jnp.arange(expert_count, dtype=jnp.int32)
    chosen = routes[:, :, None] == expert_ids[None, None, :]
    member = jnp.any(chosen, axis=1)
    portion = jnp.sum(jnp.where(chosen, weights[:, :, None], 0.0), axis=1)
    earlier = jnp.tril(jnp.ones((token_count, token_count), jnp.bfloat16), -1)
    rank = jnp.dot(earlier, member.astype(jnp.bfloat16), preferred_element_type=jnp.float32)
    slots = jnp.arange(capacity, dtype=jnp.float32)
    placed = member.T[:, None, :] & (rank.T[:, None, :] == slots[None, :, None])
    placed = placed.reshape(expert_count * capacity, token_count)
    outgoing = jnp.dot(
        placed.astype(jnp.bfloat16), hidden, preferred_element_type=jnp.float32
    ).astype(jnp.bfloat16)
    outgoing = outgoing.reshape(expert_count, capacity, column_count)
    received = quarter_to_whole(
        lax.all_to_all(outgoing, "dp", split_axis=0, concat_axis=0, tiled=True)
    )
    slot_count = received.shape[1]
    grouped = received.reshape(-1, local_experts, slot_count, received.shape[2])
    gate_act = jnp.einsum("secd,edf->secf", grouped, w_gate, preferred_element_type=jnp.float32)
    upward = jnp.einsum("secd,edf->secf", grouped, w_up, preferred_element_type=jnp.float32)
    active = (jax.nn.silu(gate_act) * upward).astype(jnp.bfloat16)
    partial_value = jnp.einsum("secf,efd->secd", active, w_down, preferred_element_type=jnp.float32)
    partial_value = partial_value.reshape(received.shape[0], slot_count, partial_value.shape[3])
    summed = sent_and_summed(partial_value.astype(jnp.bfloat16), "tp", 2)
    back = lax.all_to_all(
        summed.astype(jnp.bfloat16), "dp", split_axis=0, concat_axis=0, tiled=True
    )
    flat_back = back.reshape(expert_count * capacity, back.shape[2])
    spread = jnp.broadcast_to(portion.T[:, None, :], (expert_count, capacity, token_count))
    spread = jnp.where(placed, spread.reshape(expert_count * capacity, token_count), 0.0)
    upper = spread.astype(jnp.bfloat16)
    lower = (spread - upper.astype(jnp.float32)).astype(jnp.bfloat16)
    both = jnp.concatenate([upper, lower], axis=1)
    mixed = lax.dot_general(
        both, flat_back, (((0,), (0,)), ((), ())), preferred_element_type=jnp.float32
    )
    expert_mix = mixed[:token_count] + mixed[token_count:]
    own_out = (hidden.astype(jnp.float32) + expert_mix).astype(jnp.bfloat16)
    full_out = gathered_copies(own_out, "tp", 1)
    widened = full_out.astype(jnp.float32)
    scaling = lax.rsqrt(jnp.mean(widened * widened, axis=1, keepdims=True) + 1e-06)
    normed = (widened * scaling * norm_gain).astype(jnp.bfloat16)
    tree_key_rows = jnp.dot(
        normed, key_projection_weight, preferred_element_type=jnp.float32
    ).astype(jnp.bfloat16)
    tree_value_rows = jnp.dot(
        normed, value_projection_weight, preferred_element_type=jnp.float32
    ).astype(jnp.bfloat16)
    attended = attend_local(
        queries,
        cached_key_rows,
        cached_value_rows,
        tree_key_rows,
        tree_value_rows,
        lengths,
        parents,
    )
    return (own_out, tree_key_rows, tree_value_rows, attended)


def solution(mesh):
    return jax.shard_map(
        on_device,
        mesh=mesh,
        in_specs=(
            P("dp", "tp"),
            P("dp", None),
            P("dp", None),
            P("dp", None, "tp"),
            P("dp", None, "tp"),
            P("dp", "tp", None),
            P(),
            P(None, "tp"),
            P(None, "tp"),
            P("dp", "tp"),
            P("dp", None, "tp"),
            P("dp", None, "tp"),
            P("dp"),
            P("dp", None),
        ),
        out_specs=(P("dp", "tp"), P("dp", "tp"), P("dp", "tp"), P("dp", "tp")),
        check_vma=False,
    )
```

profile of v0, /device:TPU:2, one launch (start us, length us, event | category | flops | bytes accessed | tf_op | source)
XLA Modules:
  0.0 239.4 jit_solution(4586139410621288270)
XLA Ops:
  7.2 0.9 copy.67
  8.2 0.7 reduce_sum.57
  8.9 0.7 broadcast_divide_fusion
  10.9 1.3 fusion.5
  12.2 40.7 %all_to_all.20 = bf16[64,8,1024]{2,1,0:T(8,128)(2,1)} all-to-all(bf16[64,8,1024]{2,1,0:T(8,128)(2,1)S(1)} %fusion.5), channel_id=1, replica_groups=mesh['dp'=64,'tp'=4] {'dp'}, dimensions={0} | all-to-all | bytes 2097152 | tf_op jit(solution)/shard_map/all_to_all | solution.py:143
  52.9 47.6 %all-gather.2.cloned.1.call-done = bf16[64,8,4096]{2,1,0:T(8,128)(2,1)} async-done(((bf16[64,8,1024]{2,1,0:T(8,128)(2,1)}), bf16[64,8,4096]{2,1,0:T(8,128)(2,1)}) %all-gather.2.cloned.1.call-update) | async-done | bytes 4194320 | tf_op jit(solution)/shard_map/all_gather | solution.py:48
  100.5 6.4 %fusion.6 = f32[64,1,8,384]{3,2,0,1:T(8,128)} fusion(bf16[64,8,4096]{2,1,0:T(8,128)(2,1)} %all-gather.2.cloned.1.call-done, bf16[1,4096,384]{2,1,0:T(8,128)(2,1)} %param.17), kind=kOutput, calls=%fused_computation.9 | convolution fusion | flops 1610612736 | bytes 8126464 | tf_op jit(solution)/shard_map/secd,edf->secf/dot_general | solution.py:147
  107.0 9.7 %convolution_convert_fusion = bf16[64,8,4096]{2,1,0:T(8,128)(2,1)} fusion(bf16[1,384,4096]{2,1,0:T(8,128)(2,1)S(1)} %copy-done, bf16[64,8,4096]{2,1,0:T(8,128)(2,1)} %all-gather.2.cloned.1.call-done, bf16[1,4096,384]{2,1,0:T(8,128)(2,1)} %param.18, f32[64,1,8,384]{3,2,0,1:T(8,128)} %fusion.6), kind=kOutput, calls=%fused_computation | convolution fusion | flops 3224502272 | bytes 15466496 | tf_op jit(solution)/shard_map/secf,efd->secd/dot_general | solution.py:150
  116.7 2.6 %copy.101 = bf16[64,8,4,1024]{3,1,0,2:T(8,128)(2,1)S(1)} copy(bf16[64,8,4,1024]{3,1,2,0:T(8,128)(2,1)} %bitcast.160) | data formatting | bytes 8388608 | tf_op jit(solution)/shard_map/convert_element_type | solution.py:152
  119.3 52.5 %all_to_all.21 = bf16[4,64,8,1024]{3,2,1,0:T(8,128)(2,1)} all-to-all(bf16[4,64,8,1024]{3,2,1,0:T(8,128)(2,1)S(1)} %bitcast.157), channel_id=1, replica_groups=mesh['dp'=64,'tp'=4] {'tp'}, dimensions={0} | all-to-all | bytes 8388608 | tf_op jit(solution)/shard_map/all_to_all | solution.py:18
  171.8 4.4 %reduce_sum.59 = bf16[64,8,1024]{2,1,0:T(8,128)(2,1)} reduce(bf16[4,64,8,1024]{3,2,1,0:T(8,128)(2,1)} %all_to_all.21, bf16[]{:T(256)} %constant.15.clone.1), dimensions={0}, to_apply=%region_3.4 | reduce | flops 1572864 | bytes 5242882 | tf_op jit(solution)/shard_map/reduce_sum | solution.py:19
  176.2 10.8 %all-to-all-start.2 = ((bf16[64,8,1024]{2,1,0:T(8,128)(2,1)}), bf16[64,8,1024]{2,1,0:T(8,128)(2,1)}, u32[]{:S(2)}, u32[]{:S(2)}) async-start(bf16[64,8,1024]{2,1,0:T(8,128)(2,1)} %reduce_sum.59), calls=%async_computation.2 | async-start | bytes 2097152 | tf_op jit(solution)/shard_map/all_to_all | solution.py:153
  187.8 0.7 copy.78
  189.1 0.5 iota_compare_fusion.2
  189.7 26.1 %all-to-all-done.2 = bf16[64,8,1024]{2,1,0:T(8,128)(2,1)} async-done(((bf16[64,8,1024]{2,1,0:T(8,128)(2,1)}), bf16[64,8,1024]{2,1,0:T(8,128)(2,1)}, u32[]{:S(2)}, u32[]{:S(2)}) %all-to-all-start.2) | async-done | bytes 1048608 | tf_op jit(solution)/shard_map/all_to_all | solution.py:153
  215.8 1.6 fusion.29
  217.4 0.7 broadcast_in_dim.81
  218.1 3.4 %all-to-all-start.3 = ((bf16[4,32,1024]{2,1,0:T(8,128)(2,1)}), bf16[4,32,1024]{2,1,0:T(8,128)(2,1)S(1)}, u32[]{:S(2)}, u32[]{:S(2)}) async-start(bf16[4,32,1024]{2,1,0:T(8,128)(2,1)} %broadcast_in_dim.81), calls=%async_computation.3 | async-start | bytes 524288 | tf_op jit(solution)/shard_map/all_to_all | solution.py:30
  221.5 2.4 %fusion.71 = (f32[16,32]{1,0:T(8,128)}, f32[1,1,16,32,128]{4,3,2,1,0:T(8,128)}) fusion(bf16[1,128,128]{2,1,0:T(8,128)(2,1)} %param.24, pred[128]{0:T(512)(128)(4,1)} %iota_compare_fusion.2, bf16[32,2048]{1,0:T(8,128)(2,1)} %param.23), kind=kOutput, calls=%fused_computation.96 | convolution fusion | flops 16973312 | bytes 428160 | tf_op jit(solution)/shard_map/rnkgd,rpkd->rkgnp/dot_general | solution.py:68
  223.9 4.2 %all-to-all-done.3 = bf16[4,32,1024]{2,1,0:T(8,128)(2,1)S(1)} async-done(((bf16[4,32,1024]{2,1,0:T(8,128)(2,1)}), bf16[4,32,1024]{2,1,0:T(8,128)(2,1)S(1)}, u32[]{:S(2)}, u32[]{:S(2)}) %all-to-all-start.3) | async-done | bytes 262176 | tf_op jit(solution)/shard_map/all_to_all | solution.py:30
  228.5 1.7 convolution_convert_fusion.3
  230.9 0.3 convolution_convert_fusion.2
  231.3 0.3 convolution_bitcast_fusion
  231.9 0.7 copy.102
  (61 shorter events, 3.4 us)
Async XLA Ops:
  7.2 99.8 %copy-start = (bf16[1,384,4096]{2,1,0:T(8,128)(2,1)S(1)}, bf16[1,384,4096]{2,1,0:T(8,128)(2,1)}, u32[]{:S(2)}) copy-start(bf16[1,384,4096]{2,1,0:T(8,128)(2,1)} %param.19) | copy-start | bytes 9437188
  7.2 93.3 %all-gather.2.cloned.1.call-start = ((), (), s32[]{:S(2)}) async-start(), calls=%async_computation.4 | async-start | bytes 5242880 | tf_op jit(solution)/shard_map/all_gather | solution.py:48
  171.8 15.3 %copy-start.11 = (s32[1,32]{1,0:T(1,128)S(1)}, s32[1,32]{1,0:T(1,128)}, u32[]{:S(2)}) copy-start(s32[1,32]{1,0:T(1,128)} %param.27) | copy-start | bytes 388
  176.2 41.1 %copy-start.4 = (bf16[32,1024]{1,0:T(8,128)(2,1)S(1)}, bf16[32,1024]{1,0:T(8,128)(2,1)}, u32[]{:S(2)}) copy-start(bf16[32,1024]{1,0:T(8,128)(2,1)} %param.14) | copy-start | bytes 196612
  176.2 39.6 %all-to-all-start.2 = ((bf16[64,8,1024]{2,1,0:T(8,128)(2,1)}), bf16[64,8,1024]{2,1,0:T(8,128)(2,1)}, u32[]{:S(2)}, u32[]{:S(2)}) async-start(bf16[64,8,1024]{2,1,0:T(8,128)(2,1)} %reduce_sum.59), calls=%async_computation.2 | async-start | bytes 2097152 | tf_op jit(solution)/shard_map/all_to_all | solution.py:153
  187.0 41.4 %copy-start.6 = (f32[4096]{0:T(1024)S(1)}, f32[4096]{0:T(1024)}, u32[]{:S(2)}) copy-start(f32[4096]{0:T(1024)} %param.20) | copy-start | bytes 49156
  215.8 14.4 %copy-start.3 = (bf16[32,2048]{1,0:T(8,128)(2,1)S(1)}, bf16[32,2048]{1,0:T(8,128)(2,1)}, u32[]{:S(2)}) copy-start(bf16[32,2048]{1,0:T(8,128)(2,1)} %param.23) | copy-start | bytes 393220
  217.4 0.7 copy-start.5
  218.1 10.1 %all-to-all-start.3 = ((bf16[4,32,1024]{2,1,0:T(8,128)(2,1)}), bf16[4,32,1024]{2,1,0:T(8,128)(2,1)S(1)}, u32[]{:S(2)}, u32[]{:S(2)}) async-start(bf16[4,32,1024]{2,1,0:T(8,128)(2,1)} %broadcast_in_dim.81), calls=%async_computation.3 | async-start | bytes 524288 | tf_op jit(solution)/shard_map/all_to_all | solution.py:30
  228.2 2.0 copy-start.9
  228.2 2.4 copy-start.8
  228.2 2.5 %copy-start.2 = (f32[1,1,16,32,128]{4,3,2,1,0:T(8,128)S(1)}, f32[1,1,16,32,128]{4,3,2,1,0:T(8,128)}, u32[]{:S(2)}) copy-start(f32[1,1,16,32,128]{4,3,2,1,0:T(8,128)} %get-tuple-element.7) | copy-start | bytes 786436
  228.2 2.7 %copy-start.1 = (bf16[4096,128]{1,0:T(8,128)(2,1)S(1)}, bf16[4096,128]{1,0:T(8,128)(2,1)}, u32[]{:S(2)}) copy-start(bf16[4096,128]{1,0:T(8,128)(2,1)} %param.22) | copy-start | bytes 3145732
  228.2 3.1 %copy-start.12 = (bf16[1,128,128]{2,1,0:T(8,128)(2,1)S(1)}, bf16[1,128,128]{2,1,0:T(8,128)(2,1)}, u32[]{:S(2)}) copy-start(bf16[1,128,128]{2,1,0:T(8,128)(2,1)} %param.25) | copy-start | bytes 98308
  230.2 2.4 %copy-start.7 = (bf16[32,128]{1,0:T(8,128)(2,1)}, bf16[32,128]{1,0:T(8,128)(2,1)S(1)}, u32[]{:S(2)}) copy-start(bf16[32,128]{1,0:T(8,128)(2,1)S(1)} %convolution_convert_fusion.3) | copy-start | bytes 24580
  231.2 1.4 copy-start.10
Sparse Core Ops, SparseCore 0:
  53.0 47.4 all-gather.1
where the time goes:
time: 240 us; the launch traced here: 239 us
  blocking collectives  93.2 us (39%)
  waiting for transfers between devices  77.9 us (32%)
  matrix products  25.2 us (10%)
  between operations  15 us (6%)
  starting transfers between devices  14.3 us (6%)
  other arithmetic  7.3 us (3%)
  local copies, waits for them, and re-layouts  6.57 us (3%)
    all_to_all x1, blocking collectives, sent_and_summed(): tiles = lax.all_to_all(split_up(shard, dim, size), axis, 0, 0, tiled=True)  52.5 us
    all_gather x1, waiting for transfers between devices, quarter_to_whole(): return lax.all_gather(received, 'tp', axis=2, tiled=True)  47.6 us
    all_to_all x1, blocking collectives, on_device(): lax.all_to_all(outgoing, 'dp', split_axis=0, concat_axis=0, tiled=True)  40.7 us
    all_to_all x1, waiting for transfers between devices, on_device(): lax.all_to_all(summed.astype(jnp.bfloat16), 'dp', split_axis=0, concat_ax...  26.1 us
    all_to_all x1, starting transfers between devices, on_device(): lax.all_to_all(summed.astype(jnp.bfloat16), 'dp', split_axis=0, concat_ax...  10.8 us
    dot_general x1, matrix products, on_device(): jnp.einsum('secf,efd->secd', active, w_down, preferred_element_type=jnp.f...  9.74 us
    dot_general x1, matrix products, on_device(): jnp.einsum('secd,edf->secf', grouped, w_gate, preferred_element_type=jnp....  6.43 us
  transfers between devices with their start and end apart: 3, of which 3 were waited for; matrix products, arithmetic and copies ran while one was open for 2% of the time, Pallas kernels for 0%

commit v1 on v0

--- a/solution.py
+++ b/solution.py
@@ -5,6 +5,11 @@
 from jax.sharding import PartitionSpec as P
 
 HEAD_SIZE = 128
+
+
+def swapped_in(array, mesh_axis, dim):
+    outgoing = jnp.stack([array] * lax.axis_size(mesh_axis))
+    return jnp.concatenate(lax.all_to_all(outgoing, mesh_axis, 0, 0), axis=dim)
 
 
 def split_up(shard, dim, size):
@@ -45,7 +50,7 @@
 
 
 def quarter_to_whole(received):
-    return lax.all_gather(received, "tp", axis=2, tiled=True)
+    return swapped_in(received, "tp", 2)
 
 
 def attend_local(

time: 240 us -> 227 us (0.946)
  blocking collectives: 93.2 us -> 143 us
  waiting for transfers between devices: 77.9 us -> 32 us
  between operations: 15 us -> 1.62 us
  matrix products: 25.2 us -> 22.2 us
  local copies, waits for them, and re-layouts: 6.57 us -> 9.07 us
  starting transfers between devices: 14.3 us -> 11.8 us
    all_to_all x0 -> x1, blocking collectives: none -> 52.1 us  [swapped_in(): return jnp.concatenate(lax.all_to_all(outgoing, mesh_axis, 0, 0), axis=dim)]
    all_gather x1 -> x0, waiting for transfers between devices: 47.6 us -> none  [quarter_to_whole(): return lax.all_gather(received, 'tp', axis=2, tiled=True)]
    dot_general x1, matrix products: 6.43 us -> 3.26 us  [on_device(): jnp.einsum('secd,edf->secf', grouped, w_gate, preferred_element_type=jnp....]
    all_to_all x1, starting transfers between devices: 10.8 us -> 8.35 us  [on_device(): lax.all_to_all(summed.astype(jnp.bfloat16), 'dp', split_axis=0, concat_ax...]
    all_to_all x1, blocking collectives: 52.5 us -> 50 us  [sent_and_summed(): tiles = lax.all_to_all(split_up(shard, dim, size), axis, 0, 0, tiled=True)]
  transfers between devices with their start and end apart: 3 -> 2, of which waited for: 3 -> 2; matrix products, arithmetic and copies ran while one was open for 2% -> 1% of each run, Pallas kernels for 0% -> 0%
where the time goes in v1:
time: 227 us; the launch traced here: 226 us
  blocking collectives  143 us (63%)
  waiting for transfers between devices  32 us (14%)
  matrix products  22.2 us (10%)
  starting transfers between devices  11.8 us (5%)
  local copies, waits for them, and re-layouts  9.07 us (4%)
  other arithmetic  6.82 us (3%)
    all_to_all x1, blocking collectives, swapped_in(): return jnp.concatenate(lax.all_to_all(outgoing, mesh_axis, 0, 0), axis=dim)  52.1 us
    all_to_all x1, blocking collectives, sent_and_summed(): tiles = lax.all_to_all(split_up(shard, dim, size), axis, 0, 0, tiled=True)  50 us
    all_to_all x1, blocking collectives, on_device(): lax.all_to_all(outgoing, 'dp', split_axis=0, concat_axis=0, tiled=True)  40.6 us
    all_to_all x1, waiting for transfers between devices, on_device(): lax.all_to_all(summed.astype(jnp.bfloat16), 'dp', split_axis=0, concat_ax...  27.2 us
    dot_general x1, matrix products, on_device(): jnp.einsum('secf,efd->secd', active, w_down, preferred_element_type=jnp.f...  9.73 us
    all_to_all x1, starting transfers between devices, on_device(): lax.all_to_all(summed.astype(jnp.bfloat16), 'dp', split_axis=0, concat_ax...  8.35 us
    all_to_all x1, waiting for transfers between devices, copy_for_each(): return lax.all_to_all(copies, axis, split_axis=0, concat_axis=0, tiled=True)  4.84 us
  transfers between devices with their start and end apart: 2, of which 2 were waited for; matrix products, arithmetic and copies ran while one was open for 1% of the time, Pallas kernels for 0%

profile of v1, /device:TPU:2, one launch (start us, length us, event | category | flops | bytes accessed | tf_op | source)
XLA Modules:
  0.0 226.2 jit_solution(8867648091934484067)
XLA Ops:
  0.7 0.9 copy.70
  1.6 0.7 reduce_sum.57
  2.3 0.7 broadcast_divide_fusion
  4.3 1.3 fusion.5
  5.6 40.6 %all_to_all.25 = bf16[64,8,1024]{2,1,0:T(8,128)(2,1)S(1)} all-to-all(bf16[64,8,1024]{2,1,0:T(8,128)(2,1)S(1)} %fusion.5), channel_id=1, replica_groups=mesh['dp'=64,'tp'=4] {'dp'}, dimensions={0} | all-to-all | bytes 2097152 | tf_op jit(solution)/shard_map/all_to_all | solution.py:148
  46.2 0.5 stack.2
  46.8 52.1 %all_to_all.26 = bf16[4,64,8,1024]{3,2,1,0:T(8,128)(2,1)S(1)} all-to-all(bf16[4,64,8,1024]{3,2,1,0:T(8,128)(2,1)S(1)} %stack.2), channel_id=1, replica_groups=mesh['dp'=64,'tp'=4] {'tp'}, dimensions={0} | all-to-all | bytes 8388608 | tf_op jit(solution)/shard_map/all_to_all | solution.py:12
  98.8 0.6 copy.78
  99.5 1.9 copy-done.1
  101.4 3.3 %fusion.6 = f32[64,1,8,384]{3,2,0,1:T(8,128)} fusion(bf16[64,8,4096]{2,1,0:T(8,128)(2,1)S(1)} %bitcast.163, bf16[1,4096,384]{2,1,0:T(8,128)(2,1)S(1)} %copy-done.11), kind=kOutput, calls=%fused_computation.9 | convolution fusion | flops 1610612736 | bytes 8126464 | tf_op jit(solution)/shard_map/secd,edf->secf/dot_general | solution.py:152
  104.7 9.7 %convolution_convert_fusion = bf16[64,8,4096]{2,1,0:T(8,128)(2,1)} fusion(bf16[1,384,4096]{2,1,0:T(8,128)(2,1)S(1)} %copy-done, bf16[64,8,4096]{2,1,0:T(8,128)(2,1)} %bitcast.164, bf16[1,4096,384]{2,1,0:T(8,128)(2,1)} %param.18, f32[64,1,8,384]{3,2,0,1:T(8,128)} %fusion.6), kind=kOutput, calls=%fused_computation | convolution fusion | flops 3224502272 | bytes 15466496 | tf_op jit(solution)/shard_map/secf,efd->secd/dot_general | solution.py:155
  114.4 2.6 %copy.105 = bf16[64,8,4,1024]{3,1,0,2:T(8,128)(2,1)S(1)} copy(bf16[64,8,4,1024]{3,1,2,0:T(8,128)(2,1)} %bitcast.165) | data formatting | bytes 8388608 | tf_op jit(solution)/shard_map/convert_element_type | solution.py:157
  117.1 50.0 %all_to_all.27 = bf16[4,64,8,1024]{3,2,1,0:T(8,128)(2,1)} all-to-all(bf16[4,64,8,1024]{3,2,1,0:T(8,128)(2,1)S(1)} %bitcast.160), channel_id=1, replica_groups=mesh['dp'=64,'tp'=4] {'tp'}, dimensions={0} | all-to-all | bytes 8388608 | tf_op jit(solution)/shard_map/all_to_all | solution.py:23
  167.1 4.4 %reduce_sum.59 = bf16[64,8,1024]{2,1,0:T(8,128)(2,1)} reduce(bf16[4,64,8,1024]{3,2,1,0:T(8,128)(2,1)} %all_to_all.27, bf16[]{:T(256)} %constant.15.clone.1), dimensions={0}, to_apply=%region_3.4 | reduce | flops 1572864 | bytes 5242882 | tf_op jit(solution)/shard_map/reduce_sum | solution.py:24
  171.5 8.4 %all-to-all-start.3 = ((bf16[64,8,1024]{2,1,0:T(8,128)(2,1)}), bf16[64,8,1024]{2,1,0:T(8,128)(2,1)}, u32[]{:S(2)}, u32[]{:S(2)}) async-start(bf16[64,8,1024]{2,1,0:T(8,128)(2,1)} %reduce_sum.59), calls=%async_computation.3 | async-start | bytes 2097152 | tf_op jit(solution)/shard_map/all_to_all | solution.py:158
  181.4 27.2 %all-to-all-done.3 = bf16[64,8,1024]{2,1,0:T(8,128)(2,1)} async-done(((bf16[64,8,1024]{2,1,0:T(8,128)(2,1)}), bf16[64,8,1024]{2,1,0:T(8,128)(2,1)}, u32[]{:S(2)}, u32[]{:S(2)}) %all-to-all-start.3) | async-done | bytes 1048608 | tf_op jit(solution)/shard_map/all_to_all | solution.py:158
  208.6 1.5 fusion.29
  210.2 0.7 broadcast_in_dim.81
  210.9 3.4 %all-to-all-start.4 = ((bf16[4,32,1024]{2,1,0:T(8,128)(2,1)}), bf16[4,32,1024]{2,1,0:T(8,128)(2,1)S(1)}, u32[]{:S(2)}, u32[]{:S(2)}) async-start(bf16[4,32,1024]{2,1,0:T(8,128)(2,1)} %broadcast_in_dim.81), calls=%async_computation.4 | async-start | bytes 524288 | tf_op jit(solution)/shard_map/all_to_all | solution.py:35
  214.3 1.8 fusion.71
  216.1 4.8 %all-to-all-done.4 = bf16[4,32,1024]{2,1,0:T(8,128)(2,1)S(1)} async-done(((bf16[4,32,1024]{2,1,0:T(8,128)(2,1)}), bf16[4,32,1024]{2,1,0:T(8,128)(2,1)S(1)}, u32[]{:S(2)}, u32[]{:S(2)}) %all-to-all-start.4) | async-done | bytes 262176 | tf_op jit(solution)/shard_map/all_to_all | solution.py:35
  221.2 1.7 convolution_convert_fusion.3
  222.9 1.2 fusion.72
  225.5 0.7 copy.106
  (61 shorter events, 3.7 us)
Async XLA Ops:
  0.6 104.1 %copy-start = (bf16[1,384,4096]{2,1,0:T(8,128)(2,1)S(1)}, bf16[1,384,4096]{2,1,0:T(8,128)(2,1)}, u32[]{:S(2)}) copy-start(bf16[1,384,4096]{2,1,0:T(8,128)(2,1)} %param.19) | copy-start | bytes 9437188
  98.8 2.6 %copy-start.11 = (bf16[1,4096,384]{2,1,0:T(8,128)(2,1)S(1)}, bf16[1,4096,384]{2,1,0:T(8,128)(2,1)}, u32[]{:S(2)}) copy-start(bf16[1,4096,384]{2,1,0:T(8,128)(2,1)} %param.17) | copy-start | bytes 9437188
  99.5 1.9 copy-start.1
  167.1 12.8 %copy-start.10 = (s32[1,32]{1,0:T(1,128)S(1)}, s32[1,32]{1,0:T(1,128)}, u32[]{:S(2)}) copy-start(s32[1,32]{1,0:T(1,128)} %param.27) | copy-start | bytes 388
  167.1 43.0 %copy-start.4 = (bf16[32,1024]{1,0:T(8,128)(2,1)S(1)}, bf16[32,1024]{1,0:T(8,128)(2,1)}, u32[]{:S(2)}) copy-start(bf16[32,1024]{1,0:T(8,128)(2,1)} %param.14) | copy-start | bytes 196612
  167.1 47.2 %copy-start.8 = (bf16[1,128,128]{2,1,0:T(8,128)(2,1)S(1)}, bf16[1,128,128]{2,1,0:T(8,128)(2,1)}, u32[]{:S(2)}) copy-start(bf16[1,128,128]{2,1,0:T(8,128)(2,1)} %param.24) | copy-start | bytes 98308
  171.5 49.7 %copy-start.6 = (f32[4096]{0:T(1024)S(1)}, f32[4096]{0:T(1024)}, u32[]{:S(2)}) copy-start(f32[4096]{0:T(1024)} %param.20) | copy-start | bytes 49156
  171.5 37.1 %all-to-all-start.3 = ((bf16[64,8,1024]{2,1,0:T(8,128)(2,1)}), bf16[64,8,1024]{2,1,0:T(8,128)(2,1)}, u32[]{:S(2)}, u32[]{:S(2)}) async-start(bf16[64,8,1024]{2,1,0:T(8,128)(2,1)} %reduce_sum.59), calls=%async_computation.3 | async-start | bytes 2097152 | tf_op jit(solution)/shard_map/all_to_all | solution.py:158
  210.1 15.1 %copy-start.5 = (bf16[32,1024]{1,0:T(8,128)(2,1)}, bf16[32,1024]{1,0:T(8,128)(2,1)S(1)}, u32[]{:S(2)}) copy-start(bf16[32,1024]{1,0:T(8,128)(2,1)S(1)} %fusion.40) | copy-start | bytes 196612
  210.9 10.1 %all-to-all-start.4 = ((bf16[4,32,1024]{2,1,0:T(8,128)(2,1)}), bf16[4,32,1024]{2,1,0:T(8,128)(2,1)S(1)}, u32[]{:S(2)}, u32[]{:S(2)}) async-start(bf16[4,32,1024]{2,1,0:T(8,128)(2,1)} %broadcast_in_dim.81), calls=%async_computation.4 | async-start | bytes 524288 | tf_op jit(solution)/shard_map/all_to_all | solution.py:35
  220.9 3.3 %copy-start.3 = (f32[1,1,16,32,128]{4,3,2,1,0:T(8,128)S(1)}, f32[1,1,16,32,128]{4,3,2,1,0:T(8,128)}, u32[]{:S(2)}) copy-start(f32[1,1,16,32,128]{4,3,2,1,0:T(8,128)} %get-tuple-element.7) | copy-start | bytes 786436
  220.9 3.6 %copy-start.2 = (bf16[4096,128]{1,0:T(8,128)(2,1)S(1)}, bf16[4096,128]{1,0:T(8,128)(2,1)}, u32[]{:S(2)}) copy-start(bf16[4096,128]{1,0:T(8,128)(2,1)} %param.22) | copy-start | bytes 3145732
  220.9 3.9 %copy-start.12 = (bf16[1,128,128]{2,1,0:T(8,128)(2,1)S(1)}, bf16[1,128,128]{2,1,0:T(8,128)(2,1)}, u32[]{:S(2)}) copy-start(bf16[1,128,128]{2,1,0:T(8,128)(2,1)} %param.25) | copy-start | bytes 98308
  222.9 3.3 %copy-start.7 = (bf16[32,128]{1,0:T(8,128)(2,1)}, bf16[32,128]{1,0:T(8,128)(2,1)S(1)}, u32[]{:S(2)}) copy-start(bf16[32,128]{1,0:T(8,128)(2,1)S(1)} %convolution_convert_fusion.3) | copy-start | bytes 24580
  224.9 1.4 copy-start.9
